TPU v7x, 512 devices: a whole 4x8x8 slice. The times are simulated.
512 devices in a mesh: tm: 32 (over z, y_hi, core), space: 16 (over x, y_lo).
Axes of the slice: x: 4, y: 8 (y_hi: 2, y_lo: 4; y = y_hi * 4 + y_lo), z: 8, core: 2. Of those that a mesh axis runs over, the one named last changes fastest.
Arguments:
- q_spatial: bfloat16 [64, 1024, 1152], P('tm', 'space'), may hold values from -40 to 40
- k_spatial: bfloat16 [64, 1024, 1152], P('tm', 'space'), may hold values from -40 to 40
- v_spatial: bfloat16 [64, 1024, 1152], P('tm', 'space'), may hold values from -6 to 6
- stream: bfloat16 [64, 1024, 1152], P('tm', 'space'), may hold values from -6 to 6
- q_temporal: bfloat16 [64, 1024, 1152], P('tm', 'space'), may hold values from -40 to 40
- k_temporal: bfloat16 [64, 1024, 1152], P('tm', 'space'), may hold values from -40 to 40
Outputs:
- spatial_out: bfloat16 [64, 1024, 1152], P('tm', 'space')
- temporal_out: bfloat16 [64, 1024, 1152], P('tm', 'space')
All inputs are finite; a program needn't handle non-finite values.
Results may differ from a plain program's by a relative error of at most 0.0053.
Values may be sent and summed in bfloat16 or wider, within the bound.
A program may use at most 64 MiB of HBM per device.

v0:
```python
import jax
import jax.numpy as jnp
from jax import lax
from jax.sharding import PartitionSpec as P

D = 1152
HEADS = 16


def absorb_block(carry, queries, key_block, value_block, score_scale):
    maxima, totals, running = carry
    head_size = D // HEADS
    local_rows = queries.shape[0]
    block_rows = key_block.shape[0]
    q_heads = queries.reshape(local_rows, HEADS, head_size)
    k_heads = key_block.reshape(block_rows, HEADS, head_size)
    v_heads = value_block.reshape(block_rows, HEADS, head_size)
    scores = (
        jnp.einsum("qhd,khd->hqk", q_heads, k_heads, preferred_element_type=jnp.float32)
        * score_scale
    )
    new_maxima = jnp.maximum(maxima, jnp.max(scores, axis=-1))
    rescale = jnp.exp(maxima - new_maxima)
    raised = jnp.exp(scores - new_maxima[:, :, None])
    totals = totals * rescale + jnp.sum(raised, axis=-1)
    mixed = jnp.einsum(
        "hqk,khd->qhd", raised.astype(jnp.bfloat16), v_heads, preferred_element_type=jnp.float32
    )
    running = running * jnp.transpose(rescale)[:, :, None] + mixed
    return (new_maxima, totals, running)


def per_device(q_spatial, k_spatial, v_spatial, stream, q_temporal, k_temporal):
    head_size = D // HEADS
    score_scale = 1.0 / head_size**0.5
    frame_here = q_spatial.shape[0]
    local_rows = q_spatial.shape[1]
    initial = tuple(
        (
            (
                jnp.full((HEADS, local_rows), -1e30, jnp.float32),
                jnp.zeros((HEADS, local_rows), jnp.float32),
                jnp.zeros((local_rows, HEADS, head_size), jnp.float32),
            )
            for frame in range(frame_here)
        )
    )
    key_piece = lax.all_gather(k_spatial, "space", axis=1, tiled=True)
    value_piece = lax.all_gather(v_spatial, "space", axis=1, tiled=True)
    piece_rows = key_piece.shape[1]
    updated = []
    for frame in range(frame_here):
        absorb_state = initial[frame]
        for offset in range(0, piece_rows, 512):
            width_now = min(512, piece_rows - offset)
            absorb_state = absorb_block(
                absorb_state,
                q_spatial[frame],
                key_piece[frame, offset : offset + width_now],
                value_piece[frame, offset : offset + width_now],
                score_scale,
            )
        updated.append(absorb_state)
    result = tuple(updated)
    spatial = jnp.stack(
        [
            (state[2] / jnp.transpose(state[1])[:, :, None]).reshape(local_rows, D)
            for state in result
        ]
    ).astype(jnp.bfloat16)
    values_t = (stream.astype(jnp.float32) + spatial.astype(jnp.float32)).astype(jnp.bfloat16)
    q_pos, k_pos, v_pos = (
        lax.all_to_all(q_temporal, "tm", split_axis=1, concat_axis=0, tiled=True),
        lax.all_to_all(k_temporal, "tm", split_axis=1, concat_axis=0, tiled=True),
        lax.all_to_all(values_t, "tm", split_axis=1, concat_axis=0, tiled=True),
    )
    frame_count = q_pos.shape[0]
    positions = q_pos.shape[1]
    q_heads = q_pos.reshape(frame_count, positions, HEADS, head_size)
    k_heads = k_pos.reshape(frame_count, positions, HEADS, head_size)
    v_heads = v_pos.reshape(frame_count, positions, HEADS, head_size)
    scores = (
        jnp.einsum("fphd,gphd->phfg", q_heads, k_heads, preferred_element_type=jnp.float32)
        * score_scale
    )
    maxima = jnp.max(scores, axis=-1, keepdims=True)
    raised = jnp.exp(scores - maxima)
    totals = jnp.sum(raised, axis=-1)
    mixed = jnp.einsum(
        "phfg,gphd->fphd", raised.astype(jnp.bfloat16), v_heads, preferred_element_type=jnp.float32
    )
    mixed = mixed / jnp.transpose(totals, (2, 0, 1))[:, :, :, None]
    temporal_pos = mixed.reshape(frame_count, positions, D).astype(jnp.bfloat16)
    temporal = lax.all_to_all(temporal_pos, "tm", split_axis=0, concat_axis=1, tiled=True)
    return (spatial, temporal)


def solution(mesh):
    return jax.shard_map(
        per_device,
        mesh=mesh,
        in_specs=(
            P("tm", "space", None),
            P("tm", "space", None),
            P("tm", "space", None),
            P("tm", "space", None),
            P("tm", "space", None),
            P("tm", "space", None),
        ),
        out_specs=(P("tm", "space", None), P("tm", "space", None)),
        check_vma=False,
    )
```

profile of v0, /device:TPU:1, one launch (start us, length us, event | category | flops | bytes accessed | tf_op | source)
XLA Modules:
  0.0 361.4 jit_solution(7621973641516589648)
XLA Ops:
  8.7 2.0 copy.81
  10.6 17.3 %all-to-all-start.1 = ((bf16[2,64,1152]{2,0,1:T(2,128)(2,1)}), bf16[2,64,1152]{2,0,1:T(2,128)(2,1)}, u32[]{:S(2)}, u32[]{:S(2)}) async-start(bf16[2,64,1152]{2,0,1:T(2,128)(2,1)} %copy.81), calls=%async_computation.1 | async-start | bytes 589824 | tf_op jit(solution)/shard_map/all_to_all | solution.py:73
  27.9 2.0 copy.83
  32.3 101.3 %all-gather.3.cloned.1.call-done = bf16[2,1024,1152]{2,1,0:T(8,128)(2,1)} async-done(((bf16[2,64,1152]{2,1,0:T(8,128)(2,1)}), bf16[2,1024,1152]{2,1,0:T(8,128)(2,1)}) %all-gather.3.cloned.1.call-update) | async-done | bytes 4718608 | tf_op jit(solution)/shard_map/all_gather | solution.py:48
  133.5 4.1 %fusion.64 = (bf16[1,512,1152]{2,1,0:T(8,128)(2,1)S(1)}, bf16[1,512,1152]{2,1,0:T(8,128)(2,1)S(1)}, bf16[1,512,1152]{2,1,0:T(8,128)(2,1)}, bf16[1,512,1152]{2,1,0:T(8,128)(2,1)}) fusion(bf16[2,1024,1152]{2,1,0:T(8,128)(2,1)} %all-gather.3.cloned.1.call-done), kind=kLoop, calls=%fused_computation.88 | loop fusion | bytes 9437184 | tf_op jit(solution)/shard_map/slice | solution.py:59
  137.7 1.5 copy.75
  139.2 109.9 %all-gather.5.cloned.1.call-done = bf16[2,1024,1152]{2,1,0:T(8,128)(2,1)} async-done(((bf16[2,64,1152]{2,1,0:T(8,128)(2,1)}), bf16[2,1024,1152]{2,1,0:T(8,128)(2,1)}) %all-gather.5.cloned.1.call-update) | async-done | bytes 4718608 | tf_op jit(solution)/shard_map/all_gather | solution.py:49
  249.0 4.1 %fusion.63 = (bf16[1,512,1152]{2,1,0:T(8,128)(2,1)}, bf16[1,512,1152]{2,1,0:T(8,128)(2,1)}, bf16[1,512,1152]{2,1,0:T(8,128)(2,1)S(1)}, bf16[1,512,1152]{2,1,0:T(8,128)(2,1)S(1)}) fusion(bf16[2,1024,1152]{2,1,0:T(8,128)(2,1)} %all-gather.5.cloned.1.call-done), kind=kLoop, calls=%fused_computation.87 | loop fusion | bytes 9437184 | tf_op jit(solution)/shard_map/slice | solution.py:60
  253.1 2.4 copy.77
  255.5 2.4 copy.74
  258.0 1.5 copy.67
  259.4 1.5 copy.72
  260.9 2.8 multiply_reduce_fusion
  264.2 2.5 copy.68
  266.7 2.5 copy.65
  269.2 1.9 multiply_reduce_fusion.2
  271.6 1.8 copy-done.2
  278.6 1.5 fusion.14
  282.1 2.1 fusion.19
  284.7 10.7 %all-to-all-start.2 = ((bf16[2,64,1152]{2,0,1:T(2,128)(2,1)}), bf16[2,64,1152]{2,0,1:T(2,128)(2,1)S(1)}, u32[]{:S(2)}, u32[]{:S(2)}) async-start(bf16[2,64,1152]{2,0,1:T(2,128)(2,1)} %copy.83), calls=%async_computation.2 | async-start | bytes 589824 | tf_op jit(solution)/shard_map/all_to_all | solution.py:74
  296.5 12.8 %all-to-all-done.2 = bf16[2,64,1152]{2,0,1:T(2,128)(2,1)S(1)} async-done(((bf16[2,64,1152]{2,0,1:T(2,128)(2,1)}), bf16[2,64,1152]{2,0,1:T(2,128)(2,1)S(1)}, u32[]{:S(2)}, u32[]{:S(2)}) %all-to-all-start.2) | async-done | bytes 294944 | tf_op jit(solution)/shard_map/all_to_all | solution.py:74
  309.3 6.7 %all-to-all-start = ((bf16[2,64,1152]{2,0,1:T(2,128)(2,1)}), bf16[2,64,1152]{2,0,1:T(2,128)(2,1)S(1)}, u32[]{:S(2)}, u32[]{:S(2)}) async-start(bf16[2,64,1152]{2,0,1:T(2,128)(2,1)} %copy.79), calls=%async_computation | async-start | bytes 589824 | tf_op jit(solution)/shard_map/all_to_all | solution.py:75
  320.4 9.5 %all-to-all-done = bf16[2,64,1152]{2,0,1:T(2,128)(2,1)S(1)} async-done(((bf16[2,64,1152]{2,0,1:T(2,128)(2,1)}), bf16[2,64,1152]{2,0,1:T(2,128)(2,1)S(1)}, u32[]{:S(2)}, u32[]{:S(2)}) %all-to-all-start) | async-done | bytes 294944 | tf_op jit(solution)/shard_map/all_to_all | solution.py:75
  333.1 20.4 %all_to_all.63 = bf16[64,2,1152]{2,1,0:T(2,128)(2,1)S(1)} all-to-all(bf16[64,2,1152]{2,1,0:T(2,128)(2,1)S(1)} %reshape.45), channel_id=1, replica_groups=mesh['tm'=32,'space'=16] {'tm'}, dimensions={0} | all-to-all | bytes 589824 | tf_op jit(solution)/shard_map/all_to_all | solution.py:94
  (67 shorter events, 22.0 us)
Async XLA Ops:
  7.2 22.8 %copy-start.13 = (bf16[2,64,1152]{2,1,0:T(8,128)(2,1)S(1)}, bf16[2,64,1152]{2,1,0:T(8,128)(2,1)}, u32[]{:S(2)}) copy-start(bf16[2,64,1152]{2,1,0:T(8,128)(2,1)} %param.6) | copy-start | bytes 884740
  7.2 126.4 %all-gather.3.cloned.1.call-start = ((), (), s32[]{:S(2)}) async-start(), calls=%async_computation.4 | async-start | bytes 5013504 | tf_op jit(solution)/shard_map/all_gather | solution.py:48
  7.9 241.1 %all-gather.5.cloned.1.call-start = ((), (), s32[]{:S(2)}) async-start(), calls=%async_computation.5 | async-start | bytes 5013504 | tf_op jit(solution)/shard_map/all_gather | solution.py:49
  10.6 274.1 %all-to-all-start.1 = ((bf16[2,64,1152]{2,0,1:T(2,128)(2,1)}), bf16[2,64,1152]{2,0,1:T(2,128)(2,1)}, u32[]{:S(2)}, u32[]{:S(2)}) async-start(bf16[2,64,1152]{2,0,1:T(2,128)(2,1)} %copy.81), calls=%async_computation.1 | async-start | bytes 589824 | tf_op jit(solution)/shard_map/all_to_all | solution.py:73
  259.4 1.5 copy-start.3
  260.9 2.8 copy-start.4
  260.9 2.8 copy-start.9
  264.2 4.9 %copy-start.8 = (bf16[64,16,72]{2,1,0:T(8,128)(2,1)S(1)}, bf16[64,16,72]{2,1,0:T(8,128)(2,1)}, u32[]{:S(2)}) copy-start(bf16[64,16,72]{2,1,0:T(8,128)(2,1)} %reshape_squeeze.32) | copy-start | bytes 442372
  269.2 1.9 copy-start.5
  271.1 3.7 %copy-start = (f32[16,64,512]{2,1,0:T(8,128)}, f32[16,64,512]{2,1,0:T(8,128)S(1)}, u32[]{:S(2)}) copy-start(f32[16,64,512]{2,1,0:T(8,128)S(1)} %get-tuple-element.27) | copy-start | bytes 6291460
  271.1 2.3 copy-start.2
  274.7 1.3 copy-start.7
  276.0 1.3 copy-start.10
  277.3 1.3 copy-start.6
  280.1 2.0 copy-start.1
  284.2 11.2 %copy-start.12 = (bf16[2,64,1152]{2,1,0:T(8,128)(2,1)S(1)}, bf16[2,64,1152]{2,1,0:T(8,128)(2,1)}, u32[]{:S(2)}) copy-start(bf16[2,64,1152]{2,1,0:T(8,128)(2,1)} %param.9) | copy-start | bytes 884740
  284.7 24.6 %all-to-all-start.2 = ((bf16[2,64,1152]{2,0,1:T(2,128)(2,1)}), bf16[2,64,1152]{2,0,1:T(2,128)(2,1)S(1)}, u32[]{:S(2)}, u32[]{:S(2)}) async-start(bf16[2,64,1152]{2,0,1:T(2,128)(2,1)} %copy.83), calls=%async_computation.2 | async-start | bytes 589824 | tf_op jit(solution)/shard_map/all_to_all | solution.py:74
  295.4 24.2 %copy-start.11 = (bf16[2,64,1152]{2,1,0:T(8,128)(2,1)}, bf16[2,64,1152]{2,1,0:T(8,128)(2,1)S(1)}, u32[]{:S(2)}) copy-start(bf16[2,64,1152]{2,1,0:T(8,128)(2,1)S(1)} %constant_dynamic-update-slice_fusion) | copy-start | bytes 884740
  309.3 20.6 %all-to-all-start = ((bf16[2,64,1152]{2,0,1:T(2,128)(2,1)}), bf16[2,64,1152]{2,0,1:T(2,128)(2,1)S(1)}, u32[]{:S(2)}, u32[]{:S(2)}) async-start(bf16[2,64,1152]{2,0,1:T(2,128)(2,1)} %copy.79), calls=%async_computation | async-start | bytes 589824 | tf_op jit(solution)/shard_map/all_to_all | solution.py:75
Sparse Core Ops, SparseCore 0:
  10.1 123.4 all-gather.2
  135.6 113.3 all-gather.4
where the time goes:
time: 362 us; the launch traced here: 361 us
  waiting for transfers between devices  235 us (65%)
  local copies, waits for them, and re-layouts  42.2 us (12%)
  starting transfers between devices  34.7 us (10%)
  blocking collectives  20.4 us (6%)
  between operations  14.4 us (4%)
  matrix products  12 us (3%)
    all_gather x1, waiting for transfers between devices, per_device(): value_piece = lax.all_gather(v_spatial, 'space', axis=1, tiled=True)  110 us
    all_gather x1, waiting for transfers between devices, per_device(): key_piece = lax.all_gather(k_spatial, 'space', axis=1, tiled=True)  101 us
    all_to_all x1, blocking collectives, per_device(): lax.all_to_all(temporal_pos, 'tm', split_axis=0, concat_axis=1, tiled=True)  20.4 us
    all_to_all x1, starting transfers between devices, per_device(): lax.all_to_all(q_temporal, 'tm', split_axis=1, concat_axis=0, tiled=True)  17.3 us
    all_to_all x1, waiting for transfers between devices, per_device(): lax.all_to_all(k_temporal, 'tm', split_axis=1, concat_axis=0, tiled=True)  12.8 us
    slice x5, local copies, waits for them, and re-layouts, per_device(): key_piece[frame, offset:offset + width_now]  12 us
    slice x5, local copies, waits for them, and re-layouts, per_device(): value_piece[frame, offset:offset + width_now]  11.9 us
    all_to_all x1, starting transfers between devices, per_device(): lax.all_to_all(k_temporal, 'tm', split_axis=1, concat_axis=0, tiled=True)  10.7 us
  transfers between devices with their start and end apart: 5, of which 4 were waited for; matrix products, arithmetic and copies ran while one was open for 14% of the time, Pallas kernels for 0%

commit v1 on v0

v1 whole, which is shorter than its diff:
```python
import math

import jax
import jax.numpy as jnp
from jax import lax
from jax.experimental import pallas as pl
from jax.experimental.pallas import tpu as pltpu
from jax.sharding import PartitionSpec as P

D = 1152
HEADS = 16
HS = 72
LT = 9
NS = 16
NT = 32
BF = jnp.bfloat16
F32 = jnp.float32
MESH = pl.DeviceIdType.MESH
FACTOR = math.log2(math.e) / math.sqrt(HS)


def dot(a, b):
    return lax.dot_general(a, b, (((1,), (0,)), ((), ())), preferred_element_type=F32)


def dot_nt(a, b):
    return lax.dot_general(a, b, (((1,), (1,)), ((), ())), preferred_element_type=F32)


def one_hot(n, column_of_row):
    rows = lax.broadcasted_iota(jnp.int32, (n, n), 0)
    cols = lax.broadcasted_iota(jnp.int32, (n, n), 1)
    return jnp.where(cols == column_of_row(rows), 1.0, 0.0).astype(BF)


def one_hot_t(n, row_of_column):
    rows = lax.broadcasted_iota(jnp.int32, (n, n), 0)
    cols = lax.broadcasted_iota(jnp.int32, (n, n), 1)
    return jnp.where(rows == row_of_column(cols), 1.0, 0.0).astype(BF)


def bits(r, low, count):
    return (r >> low) & ((1 << count) - 1)


def frame_major(r):
    return bits(r, 6, 1) * 128 + bits(r, 7, 1) * 64 + bits(r, 0, 6)


def by_peer(r):
    return bits(r, 2, 1) * 128 + bits(r, 1, 1) * 64 + bits(r, 3, 5) * 2 + bits(r, 0, 1)


def by_position(r):
    return bits(r, 1, 5) * 8 + bits(r, 7, 1) * 4 + bits(r, 0, 1) * 2 + bits(r, 6, 1)


def kernel(
    q_ref, k_ref, v_ref, stream_ref, qt_ref, kt_ref, spatial_ref, temporal_ref,
    xt, rs, osend, orecv, qks, qkr, vs, vr, ts, tr, q_f, k_f, v_f, q_p, k_p, v_p, o_p,
    send_x, recv_x, send_o, recv_o, send_qk, recv_qk, send_v, recv_v, send_t, recv_t, local,
):
    s = lax.axis_index("space")
    t = lax.axis_index("tm")

    barrier = pltpu.get_barrier_semaphore()

    def greet_space(i, c):
        pl.semaphore_signal(barrier, inc=1, device_id={"space": lax.rem(s + i, NS)}, device_id_type=MESH)
        return c

    def greet_tm(i, c):
        pl.semaphore_signal(barrier, inc=1, device_id={"tm": lax.rem(t + i, NT)}, device_id_type=MESH)
        return c

    lax.fori_loop(1, NS, greet_space, 0)
    lax.fori_loop(1, NT, greet_tm, 0)

    eye = one_hot(128, lambda r: r)

    for a, ref in enumerate((q_ref, k_ref, v_ref)):
        for j in range(LT):
            block = ref[:, :, 128 * j : 128 * j + 128].reshape(128, 128)
            xt[a, 16 * j : 16 * j + 16] = dot_nt(eye, block).reshape(16, 8, 128).astype(BF)

    pl.semaphore_wait(barrier, NS + NT - 2)

    def space_x(p, at):
        return pltpu.make_async_remote_copy(
            src_ref=xt.at[:, pl.ds(9 * p, 9)], dst_ref=rs.at[at], send_sem=send_x.at[p], recv_sem=recv_x.at[at],
            device_id={"space": p}, device_id_type=MESH)

    def tm_copy(src, dst, send, recv, p, at):
        return pltpu.make_async_remote_copy(
            src_ref=src.at[p], dst_ref=dst.at[at], send_sem=send.at[p], recv_sem=recv.at[at],
            device_id={"tm": p}, device_id_type=MESH)

    def tm_start(src, dst, send, recv):
        def body(i, c):
            tm_copy(src, dst, send, recv, lax.rem(t + i, NT), t).start()
            return c

        lax.fori_loop(1, NT, body, 0)
        own = pltpu.make_async_copy(src.at[t], dst.at[t], recv.at[t])
        own.start()

    def tm_wait(src, dst, send, recv):
        def body(i, c):
            p = lax.rem(t + i, NT)
            tm_copy(src, dst, send, recv, p, p).wait()
            return c

        lax.fori_loop(1, NT, body, 0)
        pltpu.make_async_copy(src.at[t], dst.at[t], recv.at[t]).wait()

    def start_x(i, c):
        space_x(lax.rem(s + i, NS), s).start()
        return c

    lax.fori_loop(1, NS, start_x, 0)
    own_x = pltpu.make_async_copy(xt.at[:, pl.ds(9 * s, 9)], rs.at[s], local)
    own_x.start()

    to_peer = one_hot(256, by_peer)
    for j in range(LT):
        pair = jnp.concatenate(
            [ref[:, :, 128 * j : 128 * j + 128].reshape(128, 128) for ref in (qt_ref, kt_ref)], axis=0
        )
        qks[:, j] = dot(to_peer, pair).reshape(32, 8, 128).astype(BF)
    tm_start(qks, qkr, send_qk, recv_qk)

    own_x.wait()

    def wait_x(i, c):
        p = lax.rem(s + i, NS)
        space_x(p, p).wait()
        return c

    lax.fori_loop(1, NS, wait_x, 0)

    sort = one_hot_t(256, frame_major)
    sort_t = one_hot(256, frame_major)
    for i in range(NS // 2):
        pair = [rs[2 * i + m].reshape(216, 128) for m in range(2)]
        pair = jnp.concatenate(pair, axis=1)
        qv = dot(pair, sort)
        keys = dot_nt(sort_t, pair[HS : 2 * HS])
        for f in range(2):
            q_f[f, :HS, 128 * i : 128 * i + 128] = qv[:HS, 128 * f : 128 * f + 128].astype(BF)
            v_f[f, :HS, 128 * i : 128 * i + 128] = qv[2 * HS :, 128 * f : 128 * f + 128].astype(BF)
            k_f[f, 128 * i : 128 * i + 128, :HS] = keys[128 * f : 128 * f + 128].astype(BF)

    def copy_o(p, at):
        return pltpu.make_async_remote_copy(
            src_ref=osend.at[p], dst_ref=orecv.at[at], send_sem=send_o.at[p], recv_sem=recv_o.at[at],
            device_id={"space": p}, device_id_type=MESH)

    own_o = pltpu.make_async_copy(osend.at[s], orecv.at[s], local)

    def attend(i, c):
        tile = lax.rem(lax.div(s, 4) + i, 4)
        at = pl.ds(pl.multiple_of(tile * 256, 256), 256)
        mixed = []
        for f in range(2):
            scores = dot(k_f[f, :, :HS], q_f[f, :HS, at])
            top = jnp.max(scores, axis=0, keepdims=True) * FACTOR
            raised = jnp.exp2(scores * FACTOR - top)
            total = jnp.sum(raised, axis=0, keepdims=True)
            mix = dot(v_f[f, :HS, :], raised.astype(BF))
            mixed.append((mix / total).astype(BF))
        for m in range(2):
            back = dot(jnp.concatenate([x[:, 128 * m : 128 * m + 128] for x in mixed], axis=1), sort_t)
            for n in range(2):
                osend[4 * tile + 2 * m + n] = back[:, 128 * n : 128 * n + 128].reshape(9, 8, 128).astype(BF)
        for n in range(4):
            p = 4 * tile + n

            @pl.when(p != s)
            def _():
                copy_o(p, s).start()

            @pl.when(p == s)
            def _():
                own_o.start()

        return c

    lax.fori_loop(0, 4, attend, 0)

    def wait_o(i, c):
        p = lax.rem(s + i, NS)
        copy_o(p, p).wait()
        return c

    own_o.wait()
    lax.fori_loop(1, NS, wait_o, 0)

    zeros = jnp.zeros((128, 128), BF)
    for j in range(5):
        pair = []
        for n in (2 * j, 2 * j + 1):
            if n == LT:
                pair.append(zeros)
                continue
            rows = [orecv[r // 9, r % 9] for r in range(16 * n, 16 * n + 16)]
            block = dot_nt(eye, jnp.concatenate(rows, axis=0)).astype(BF)
            lanes = slice(128 * n, 128 * n + 128)
            spatial_ref[:, :, lanes] = block.reshape(2, 64, 128)
            stream = stream_ref[:, :, lanes].reshape(128, 128)
            pair.append((stream.astype(F32) + block.astype(F32)).astype(BF))
        vs[:, j] = dot(to_peer, jnp.concatenate(pair, axis=0)).reshape(32, 8, 128).astype(BF)
    tm_start(vs, vr, send_v, recv_v)

    tm_wait(qks, qkr, send_qk, recv_qk)
    to_position = one_hot(256, by_position)
    for j in range(LT):
        both = dot(to_position, qkr[:, j].reshape(256, 128)).astype(BF)
        q_p[:, 128 * j : 128 * j + 128] = both[:128]
        k_p[:, 128 * j : 128 * j + 128] = both[128:]
    tm_wait(vs, vr, send_v, recv_v)
    for j in range(5):
        both = dot(to_position, vr[:, j].reshape(256, 128)).astype(BF)
        for n in range(2):
            if 2 * j + n < LT:
                v_p[:, 128 * (2 * j + n) : 128 * (2 * j + n) + 128] = both[128 * n : 128 * n + 128]

    rows = lax.broadcasted_iota(jnp.int32, (128, 128), 0)
    cols = lax.broadcasted_iota(jnp.int32, (128, 128), 1)
    same = (rows >> 6) == (cols >> 6)
    for h in range(HEADS):
        low, high = HS * h // 128 * 128, -(-HS * (h + 1) // 128) * 128
        lane = lax.broadcasted_iota(jnp.int32, (128, high - low), 1) + low
        mine = (lane >= HS * h) & (lane < HS * (h + 1))
        keys = jnp.where(mine, k_p[:, low:high].astype(F32), 0.0).astype(BF)
        scores = jnp.where(same, dot_nt(q_p[:, low:high], keys), -jnp.inf)
        top = jnp.max(scores, axis=1, keepdims=True) * FACTOR
        raised = jnp.exp2(scores * FACTOR - top)
        total = jnp.sum(raised, axis=1, keepdims=True)
        mix = dot(raised.astype(BF), v_p[:, low:high]) / total
        o_p[:, low:high] = jnp.where(mine, mix, o_p[:, low:high])

    from_position = one_hot_t(256, by_position)
    for j in range(5):
        pair = [o_p[:, 128 * n : 128 * n + 128].astype(BF) if n < LT else zeros for n in (2 * j, 2 * j + 1)]
        ts[:, j] = dot(from_position, jnp.concatenate(pair, axis=0)).reshape(32, 8, 128).astype(BF)
    tm_start(ts, tr, send_t, recv_t)
    tm_wait(ts, tr, send_t, recv_t)
    from_peer = one_hot_t(256, by_peer)
    for j in range(5):
        both = dot(from_peer, tr[:, j].reshape(256, 128)).astype(BF)
        for n in range(2):
            if 2 * j + n < LT:
                lanes = slice(128 * (2 * j + n), 128 * (2 * j + n) + 128)
                temporal_ref[:, :, lanes] = both[128 * n : 128 * n + 128].reshape(2, 64, 128)


def per_device(*args):
    whole = jax.ShapeDtypeStruct((2, 64, D), BF)
    dma = pltpu.SemaphoreType.DMA
    vmem = pltpu.VMEM
    return pl.pallas_call(
        kernel,
        out_shape=(whole, whole),
        in_specs=[pl.BlockSpec(memory_space=vmem)] * 6,
        out_specs=(pl.BlockSpec(memory_space=vmem),) * 2,
        scratch_shapes=[
            vmem((3, 144, 8, 128), BF),
            vmem((NS, 3, 9, 8, 128), BF),
            vmem((NS, 9, 8, 128), BF),
            vmem((NS, 9, 8, 128), BF),
            vmem((NT, LT, 8, 128), BF),
            vmem((NT, LT, 8, 128), BF),
            vmem((NT, 5, 8, 128), BF),
            vmem((NT, 5, 8, 128), BF),
            vmem((NT, 5, 8, 128), BF),
            vmem((NT, 5, 8, 128), BF),
            vmem((2, 80, 1024), BF),
            vmem((2, 1024, 128), BF),
            vmem((2, 80, 1024), BF),
            vmem((128, D), BF),
            vmem((128, D), BF),
            vmem((128, D), BF),
            vmem((128, D), F32),
            *[dma((NS,))] * 4,
            *[dma((NT,))] * 6,
            dma,
        ],
        compiler_params=pltpu.CompilerParams(
            collective_id=0, has_side_effects=True, vmem_limit_bytes=48 * 2**20
        ),
        cost_estimate=pl.CostEstimate(flops=2 * 10**9, bytes_accessed=3 * 10**6, transcendentals=3 * 10**6),
        name="attention",
    )(*args)


def solution(mesh):
    spec = P("tm", "space", None)
    return jax.shard_map(
        per_device, mesh=mesh, in_specs=(spec,) * 6, out_specs=(spec, spec), check_vma=False
    )
```

time: 362 us -> 99.8 us (0.28)
  waiting for transfers between devices: 235 us -> 0 us
  Pallas kernels: 0 us -> 91.7 us
  local copies, waits for them, and re-layouts: 42.2 us -> 7.19 us
  starting transfers between devices: 34.7 us -> 0 us
  blocking collectives: 20.4 us -> 0 us
  between operations: 14.4 us -> 0.65 us
  matrix products: 12 us -> 0 us
    all_gather x2 -> x0, waiting for transfers between devices: 211 us -> none  [the longest x1 110 us: per_device(): value_piece = lax.all_gather(v_spatial, 'space', axis=1, tiled=True)]
    pallas_call x0 -> x1, Pallas kernels: none -> 91.7 us  [per_device(): pl.pallas_call(kernel, out_shape=(whole, whole), in_specs=[pl.BlockSpec(m...]
    all_to_all x3 -> x0, starting transfers between devices: 34.6 us -> none  [the longest x1 17.3 us: per_device(): lax.all_to_all(q_temporal, 'tm', split_axis=1, concat_axis=0, tiled=True)]
    slice x11 -> x0, local copies, waits for them, and re-layouts: 23.9 us -> none  [the longest x5 12 us: per_device(): key_piece[frame, offset:offset + width_now]]
    all_to_all x3 -> x0, waiting for transfers between devices: 22.3 us -> none  [the longest x1 12.8 us: per_device(): lax.all_to_all(k_temporal, 'tm', split_axis=1, concat_axis=0, tiled=True)]
    all_to_all x1 -> x0, blocking collectives: 20.4 us -> none  [per_device(): lax.all_to_all(temporal_pos, 'tm', split_axis=0, concat_axis=1, tiled=True)]
    dot_general x10 -> x0, matrix products: 12 us -> none  [the longest x4 5.71 us: absorb_block(): jnp.einsum('qhd,khd->hqk', q_heads, k_heads, preferred_element_type=jnp.f...]
    unnamed x32 -> x14, local copies, waits for them, and re-layouts: 7.63 us -> 7.19 us
  transfers between devices with their start and end apart: 5 -> 0, of which waited for: 4 -> 0; matrix products, arithmetic and copies ran while one was open for 14% -> 0% of each run, Pallas kernels for 0% -> 0%
where the time goes in v1:
time: 99.8 us; the launch traced here: 99.5 us
  Pallas kernels  91.7 us (92%)
  local copies, waits for them, and re-layouts  7.19 us (7%)
    pallas_call x1, Pallas kernels, per_device(): pl.pallas_call(kernel, out_shape=(whole, whole), in_specs=[pl.BlockSpec(m...  91.7 us
    unnamed x14, local copies, waits for them, and re-layouts  7.19 us

profile of v1, /device:TPU:1, one launch (start us, length us, event | category | flops | bytes accessed | tf_op | source)
XLA Modules:
  0.0 99.5 jit_solution(12288580931884782983)
XLA Ops:
  0.6 0.0 copy-start
  0.6 1.0 copy-done
  1.6 0.0 copy-start.1
  1.6 1.0 copy-done.1
  2.6 0.0 copy-start.2
  2.6 1.0 copy-done.2
  3.5 0.0 copy-start.3
  3.5 1.0 copy-done.3
  4.5 0.0 copy-start.4
  4.5 1.0 copy-done.4
  5.4 0.0 copy-start.5
  5.4 1.0 copy-done.5
  6.4 91.7 %attention.1 = (bf16[2,64,1152]{2,1,0:T(8,128)(2,1)S(1)}, bf16[2,64,1152]{2,1,0:T(8,128)(2,1)S(1)}) custom-call(bf16[2,64,1152]{2,1,0:T(8,128)(2,1)S(1)} %copy-done, bf16[2,64,1152]{2,1,0:T(8,128)(2,1)S(1)} %copy-done.1, bf16[2,64,1152]{2,1,0:T(8,128)(2,1)S(1)} %copy-done.2, bf16[2,64,1152]{2,1,0:T(8,128)(2,1)S(1)} %copy-done.3, ...), custom_call_target="tpu_custom_call" | custom-call | flops 2000000000 | bytes 3000000 | tf_op jit(solution)/shard_map/attention/pallas_call | solution.py:261
  98.1 0.7 copy.10
  98.8 0.7 copy.11
Async XLA Ops:
  0.6 1.0 copy-start
  1.6 1.0 copy-start.1
  2.6 1.0 copy-start.2
  3.5 1.0 copy-start.3
  4.5 1.0 copy-start.4
  5.4 1.0 copy-start.5

commit v2 on v1

v2 whole, which is shorter than its diff:
```python
import math

import jax
import jax.numpy as jnp
from jax import lax
from jax.experimental import pallas as pl
from jax.experimental.pallas import tpu as pltpu
from jax.sharding import PartitionSpec as P

D = 1152
HEADS = 16
HS = 72
LT = 9
NS = 16
NT = 32
BF = jnp.bfloat16
F32 = jnp.float32
MESH = pl.DeviceIdType.MESH
FACTOR = math.log2(math.e) / math.sqrt(HS)


def dot(a, b):
    return lax.dot_general(a, b, (((1,), (0,)), ((), ())), preferred_element_type=F32)


def dot_nt(a, b):
    return lax.dot_general(a, b, (((1,), (1,)), ((), ())), preferred_element_type=F32)


def one_hot(n, column_of_row):
    rows = lax.broadcasted_iota(jnp.int32, (n, n), 0)
    cols = lax.broadcasted_iota(jnp.int32, (n, n), 1)
    return jnp.where(cols == column_of_row(rows), 1.0, 0.0).astype(BF)


def one_hot_t(n, row_of_column):
    rows = lax.broadcasted_iota(jnp.int32, (n, n), 0)
    cols = lax.broadcasted_iota(jnp.int32, (n, n), 1)
    return jnp.where(rows == row_of_column(cols), 1.0, 0.0).astype(BF)


def others(body):
    lax.fori_loop(0, 14, body, 0)
    body(15, 0)


def bits(r, low, count):
    return (r >> low) & ((1 << count) - 1)


def frame_major(r):
    return bits(r, 6, 1) * 128 + bits(r, 7, 1) * 64 + bits(r, 0, 6)


def by_peer(r):
    return bits(r, 2, 1) * 128 + bits(r, 1, 1) * 64 + bits(r, 3, 5) * 2 + bits(r, 0, 1)


def by_position(r):
    return bits(r, 1, 5) * 8 + bits(r, 7, 1) * 4 + bits(r, 0, 1) * 2 + bits(r, 6, 1)


def kernel(
    q_hbm, k_hbm, v_hbm, stream_hbm, qt_hbm, kt_hbm, spatial_ref, temporal_ref,
    staged, xt, rs, osend, orecv, qks, qkr, vs, vr, ts, tr, q_f, k_f, v_f, q_p, k_p, v_p, o_p,
    send_x, recv_x, send_o, recv_o, send_qk, recv_qk, send_v, recv_v, send_t, recv_t, loads,
):
    s = lax.axis_index("space")
    t = lax.axis_index("tm")

    z, y, core = lax.div(t, 4), lax.rem(lax.div(t, 2), 2), lax.rem(t, 2)
    inputs = [
        pltpu.make_async_copy(ref, staged.at[n], loads.at[n])
        for n, ref in enumerate((q_hbm, k_hbm, v_hbm, qt_hbm, kt_hbm, stream_hbm))
    ]

    def other(i, side):
        k = 7 - lax.div(i, 2)
        step = lax.div(k + 1, 2) * (2 * lax.rem(k, 2) - 1)
        return 4 * lax.rem(z + (1 - 2 * core) * step + 8, 8) + 2 * side + lax.rem(core + i, 2)

    def far(i):
        return other(i, 1 - y)

    def near(i):
        return other(i, y)

    def line(i):
        m = 3 - i
        return 2 * lax.rem(lax.div(lax.rem(s, 4), 2) + lax.div(m, 2), 2) + lax.rem(s + m, 2)

    def ring(i):
        step = 2 - lax.div(i + 1, 2)
        return lax.rem(lax.div(s, 4) + step * (1 - 2 * lax.rem(i + core, 2)) + 4, 4)

    def across(i):
        return 4 * ring(lax.div(i, 4)) + line(lax.rem(i, 4))

    barrier = pltpu.get_barrier_semaphore()

    def greet(axis, peer):
        def body(i, c):
            pl.semaphore_signal(barrier, inc=1, device_id={axis: peer(i)}, device_id_type=MESH)
            return c

        return body

    lax.fori_loop(0, 16, greet("tm", far), 0)
    others(greet("tm", near))
    lax.fori_loop(0, NS - 1, greet("space", across), 0)
    for copy in inputs:
        copy.start()

    eye = one_hot(128, lambda r: r)

    for a in range(3):
        inputs[a].wait()
        for j in range(LT):
            block = staged[a, :, :, 128 * j : 128 * j + 128].reshape(128, 128)
            xt[a, 16 * j : 16 * j + 16] = dot_nt(eye, block).reshape(16, 8, 128).astype(BF)

    pl.semaphore_wait(barrier, NS + NT - 2)

    def space_x(p, at):
        return pltpu.make_async_remote_copy(
            src_ref=xt.at[:, pl.ds(9 * p, 9)], dst_ref=rs.at[at], send_sem=send_x.at[p], recv_sem=recv_x.at[at],
            device_id={"space": p}, device_id_type=MESH)

    def tm_copy(src, dst, send, recv, p, at, part=slice(None)):
        return pltpu.make_async_remote_copy(
            src_ref=src.at[p, part], dst_ref=dst.at[at, part], send_sem=send.at[p], recv_sem=recv.at[at],
            device_id={"tm": p}, device_id_type=MESH)

    def start_far(src, dst, send, recv, part=slice(None), low=0, high=16):
        def body(i, c):
            tm_copy(src, dst, send, recv, far(i), t, part).start()
            return c

        lax.fori_loop(low, high, body, 0)

    def start_near(src, dst, send, recv, part=slice(None)):
        def body(i, c):
            tm_copy(src, dst, send, recv, near(i), t, part).start()
            return c

        others(body)
        pltpu.make_async_copy(src.at[t, part], dst.at[t, part], recv.at[t]).start()

    def wait_tm(dst, recv, part=slice(None)):
        def body(p, c):
            pltpu.make_async_copy(dst.at[p, part], dst.at[p, part], recv.at[p]).wait()
            return c

        lax.fori_loop(0, NT, body, 0)

    def sent_tm(src, send, part=slice(None)):
        def body(i, c):
            p = lax.rem(t + i, NT)
            tm_copy(src, src, send, send, p, p, part).wait_send()
            return c

        lax.fori_loop(1, NT, body, 0)

    def start_x(i, c):
        space_x(across(i), s).start()
        return c

    lax.fori_loop(0, NS - 1, start_x, 0)
    pltpu.make_async_copy(xt.at[:, pl.ds(9 * s, 9)], rs.at[s], recv_x.at[s]).start()

    to_peer = one_hot(256, by_peer)
    inputs[3].wait()
    inputs[4].wait()
    for j in range(LT):
        pair = jnp.concatenate(
            [staged[n, :, :, 128 * j : 128 * j + 128].reshape(128, 128) for n in (3, 4)], axis=0
        )
        qks[:, j] = dot(to_peer, pair).reshape(32, 8, 128).astype(BF)
    start_near(qks, qkr, send_qk, recv_qk)

    def sent_x(i, c):
        p = lax.rem(s + i, NS)
        space_x(p, p).wait_send()
        return c

    lax.fori_loop(1, NS, sent_x, 0)
    start_far(qks, qkr, send_qk, recv_qk, high=8)

    sort = one_hot_t(256, frame_major)
    sort_t = one_hot(256, frame_major)

    def arrange(i, c):
        pair = lax.rem(lax.div(s, 2) + i, NS // 2)
        for m in range(2):
            p = 2 * pair + m
            pltpu.make_async_copy(rs.at[p], rs.at[p], recv_x.at[p]).wait()
        both = jnp.concatenate([rs[2 * pair + m].reshape(216, 128) for m in range(2)], axis=1)
        qv = dot(both, sort)
        keys = dot_nt(sort_t, both[HS : 2 * HS])
        at = pl.ds(pl.multiple_of(pair * 128, 128), 128)
        for f in range(2):
            q_f[f, :HS, at] = qv[:HS, 128 * f : 128 * f + 128].astype(BF)
            v_f[f, :HS, at] = qv[2 * HS :, 128 * f : 128 * f + 128].astype(BF)
            k_f[f, at, :HS] = keys[128 * f : 128 * f + 128].astype(BF)
        return c

    lax.fori_loop(0, NS // 2, arrange, 0)

    def copy_o(p, at):
        return pltpu.make_async_remote_copy(
            src_ref=osend.at[p], dst_ref=orecv.at[at], send_sem=send_o.at[p], recv_sem=recv_o.at[at],
            device_id={"space": p}, device_id_type=MESH)

    own_o = pltpu.make_async_copy(osend.at[s], orecv.at[s], recv_o.at[s])

    def attend(i, c):
        tile = ring(i)
        at = pl.ds(pl.multiple_of(tile * 256, 256), 256)
        mixed = []
        for f in range(2):
            scores = dot(k_f[f, :, :HS], q_f[f, :HS, at])
            top = jnp.max(scores, axis=0, keepdims=True) * FACTOR
            raised = jnp.exp2(scores * FACTOR - top)
            total = jnp.sum(raised, axis=0, keepdims=True)
            mix = dot(v_f[f, :HS, :], raised.astype(BF))
            mixed.append((mix / total).astype(BF))
        for m in range(2):
            back = dot(jnp.concatenate([x[:, 128 * m : 128 * m + 128] for x in mixed], axis=1), sort_t)
            for n in range(2):
                osend[4 * tile + 2 * m + n] = back[:, 128 * n : 128 * n + 128].reshape(9, 8, 128).astype(BF)
        for n in range(4):
            p = 4 * tile + line(n)

            @pl.when(p != s)
            def _():
                copy_o(p, s).start()

            @pl.when(p == s)
            def _():
                own_o.start()

        return c

    lax.fori_loop(0, 4, attend, 0)
    inputs[5].wait()

    def wait_o(p, c):
        pltpu.make_async_copy(orecv.at[p], orecv.at[p], recv_o.at[p]).wait()
        return c

    zeros = jnp.zeros((128, 128), BF)

    def pack_v(j):
        pair = []
        for n in (2 * j, 2 * j + 1):
            if n == LT:
                pair.append(zeros)
                continue
            rows = [orecv[r // 9, r % 9] for r in range(16 * n, 16 * n + 16)]
            block = dot_nt(eye, jnp.concatenate(rows, axis=0)).astype(BF)
            lanes = slice(128 * n, 128 * n + 128)
            spatial_ref[:, :, lanes] = block.reshape(2, 64, 128)
            stream = staged[5, :, :, lanes].reshape(128, 128)
            pair.append((stream.astype(F32) + block.astype(F32)).astype(BF))
        vs[:, j] = dot(to_peer, jnp.concatenate(pair, axis=0)).reshape(32, 8, 128).astype(BF)

    def unpack_v(j):
        both = dot(to_position, vr[:, j].reshape(256, 128)).astype(BF)
        for n in range(2):
            if 2 * j + n < LT:
                v_p[:, 128 * (2 * j + n) : 128 * (2 * j + n) + 128] = both[128 * n : 128 * n + 128]

    first_v, last_v = slice(0, 3), slice(3, 5)
    lax.fori_loop(0, 11, wait_o, 0)
    start_far(qks, qkr, send_qk, recv_qk, low=8)
    for j in range(3):
        pack_v(j)
    start_far(vs, vr, send_v.at[0], recv_v.at[0], first_v)
    start_near(vs, vr, send_v.at[0], recv_v.at[0], first_v)
    lax.fori_loop(11, NS, wait_o, 0)
    for j in range(3, 5):
        pack_v(j)
    start_far(vs, vr, send_v.at[1], recv_v.at[1], last_v)
    start_near(vs, vr, send_v.at[1], recv_v.at[1], last_v)

    to_position = one_hot(256, by_position)
    wait_tm(qkr, recv_qk)
    for j in range(LT):
        both = dot(to_position, qkr[:, j].reshape(256, 128)).astype(BF)
        q_p[:, 128 * j : 128 * j + 128] = both[:128]
        k_p[:, 128 * j : 128 * j + 128] = both[128:]

    rows = lax.broadcasted_iota(jnp.int32, (128, 128), 0)
    cols = lax.broadcasted_iota(jnp.int32, (128, 128), 1)
    same = (rows >> 6) == (cols >> 6)

    def head(h):
        low, high = HS * h // 128 * 128, -(-HS * (h + 1) // 128) * 128
        lane = lax.broadcasted_iota(jnp.int32, (128, high - low), 1) + low
        mine = (lane >= HS * h) & (lane < HS * (h + 1))
        keys = jnp.where(mine, k_p[:, low:high].astype(F32), 0.0).astype(BF)
        scores = jnp.where(same, dot_nt(q_p[:, low:high], keys), -jnp.inf)
        top = jnp.max(scores, axis=1, keepdims=True) * FACTOR
        raised = jnp.exp2(scores * FACTOR - top)
        total = jnp.sum(raised, axis=1, keepdims=True)
        mix = dot(raised.astype(BF), v_p[:, low:high]) / total
        o_p[:, low:high] = jnp.where(mine, mix, o_p[:, low:high])

    from_position = one_hot_t(256, by_position)

    def pack_t(j):
        pair = [o_p[:, 128 * n : 128 * n + 128].astype(BF) if n < LT else zeros for n in (2 * j, 2 * j + 1)]
        ts[:, j] = dot(from_position, jnp.concatenate(pair, axis=0)).reshape(32, 8, 128).astype(BF)

    first_t, last_t = slice(0, 2), slice(2, 5)
    wait_tm(vr, recv_v.at[0], first_v)
    for j in range(3):
        unpack_v(j)
    for h in range(8):
        head(h)
    for j in range(2):
        pack_t(j)
    start_far(ts, tr, send_t.at[0], recv_t.at[0], first_t)
    start_near(ts, tr, send_t.at[0], recv_t.at[0], first_t)
    for h in range(8, 10):
        head(h)
    wait_tm(vr, recv_v.at[1], last_v)
    for j in range(3, 5):
        unpack_v(j)
    for h in range(10, HEADS):
        head(h)
    for j in range(2, 5):
        pack_t(j)
    start_far(ts, tr, send_t.at[1], recv_t.at[1], last_t)
    start_near(ts, tr, send_t.at[1], recv_t.at[1], last_t)

    from_peer = one_hot_t(256, by_peer)

    def unpack_t(j):
        both = dot(from_peer, tr[:, j].reshape(256, 128)).astype(BF)
        for n in range(2):
            if 2 * j + n < LT:
                lanes = slice(128 * (2 * j + n), 128 * (2 * j + n) + 128)
                temporal_ref[:, :, lanes] = both[128 * n : 128 * n + 128].reshape(2, 64, 128)

    wait_tm(tr, recv_t.at[0], first_t)
    for j in range(2):
        unpack_t(j)
    wait_tm(tr, recv_t.at[1], last_t)
    for j in range(2, 5):
        unpack_t(j)

    def sent_o(i, c):
        p = lax.rem(s + i, NS)
        copy_o(p, p).wait_send()
        return c

    lax.fori_loop(1, NS, sent_o, 0)
    sent_tm(qks, send_qk)
    for n, part in enumerate((first_v, last_v)):
        sent_tm(vs, send_v.at[n], part)
    for n, part in enumerate((first_t, last_t)):
        sent_tm(ts, send_t.at[n], part)


def per_device(*args):
    whole = jax.ShapeDtypeStruct((2, 64, D), BF)
    dma = pltpu.SemaphoreType.DMA
    vmem = pltpu.VMEM
    return pl.pallas_call(
        kernel,
        out_shape=(whole, whole),
        in_specs=[pl.BlockSpec(memory_space=pltpu.HBM)] * 6,
        out_specs=(pl.BlockSpec(memory_space=vmem),) * 2,
        scratch_shapes=[
            vmem((6, 2, 64, D), BF),
            vmem((3, 144, 8, 128), BF),
            vmem((NS, 3, 9, 8, 128), BF),
            vmem((NS, 9, 8, 128), BF),
            vmem((NS, 9, 8, 128), BF),
            vmem((NT, LT, 8, 128), BF),
            vmem((NT, LT, 8, 128), BF),
            vmem((NT, 5, 8, 128), BF),
            vmem((NT, 5, 8, 128), BF),
            vmem((NT, 5, 8, 128), BF),
            vmem((NT, 5, 8, 128), BF),
            vmem((2, 80, 1024), BF),
            vmem((2, 1024, 128), BF),
            vmem((2, 80, 1024), BF),
            vmem((128, D), BF),
            vmem((128, D), BF),
            vmem((128, D), BF),
            vmem((128, D), F32),
            *[dma((NS,))] * 4,
            *[dma((NT,))] * 2,
            *[dma((2, NT))] * 4,
            dma((6,)),
        ],
        compiler_params=pltpu.CompilerParams(
            collective_id=0, has_side_effects=True, vmem_limit_bytes=60 * 2**20
        ),
        cost_estimate=pl.CostEstimate(flops=2 * 10**9, bytes_accessed=3 * 10**6, transcendentals=3 * 10**6),
        name="attention",
    )(*args)


def solution(mesh):
    spec = P("tm", "space", None)
    return jax.shard_map(
        per_device, mesh=mesh, in_specs=(spec,) * 6, out_specs=(spec, spec), check_vma=False
    )
```

time: 99.8 us -> 90.8 us (0.910)
  local copies, waits for them, and re-layouts: 7.19 us -> 2.46 us
  Pallas kernels: 91.7 us -> 87.5 us
    unnamed x14 -> x4, local copies, waits for them, and re-layouts: 7.19 us -> 2.46 us
    pallas_call x1, Pallas kernels: 91.7 us -> 87.5 us  [per_device(): pl.pallas_call(kernel, out_shape=(whole, whole), in_specs=[pl.BlockSpec(m...]
where the time goes in v2:
time: 90.8 us; the launch traced here: 90.6 us
  Pallas kernels  87.5 us (96%)
  local copies, waits for them, and re-layouts  2.46 us (3%)
    pallas_call x1, Pallas kernels, per_device(): pl.pallas_call(kernel, out_shape=(whole, whole), in_specs=[pl.BlockSpec(m...  87.5 us
    unnamed x4, local copies, waits for them, and re-layouts  2.46 us

profile of v2, /device:TPU:1, one launch (start us, length us, event | category | flops | bytes accessed | tf_op | source)
XLA Modules:
  0.0 90.6 jit_solution(5953884976987882052)
XLA Ops:
  0.6 87.5 %attention.1 = (bf16[2,64,1152]{2,1,0:T(8,128)(2,1)}, bf16[2,64,1152]{2,1,0:T(8,128)(2,1)}) custom-call(bf16[2,64,1152]{2,1,0:T(8,128)(2,1)} %q_hbm.1, bf16[2,64,1152]{2,1,0:T(8,128)(2,1)} %k_hbm.1, bf16[2,64,1152]{2,1,0:T(8,128)(2,1)} %v_hbm.1, bf16[2,64,1152]{2,1,0:T(8,128)(2,1)} %stream_hbm.1, bf16[2,64,1152]{2,1,0:T(8,128)(2,1)} %qt_hbm.1, ...), custom_call_target="tpu_custom_call" | custom-call | flops 2000000000 | bytes 3000000 | tf_op jit(solution)/shard_map/attention/pallas_call | solution.py:370
  88.1 0.0 copy-start
  88.1 1.7 %copy.10 = bf16[2,64,1152]{2,1,0:T(8,128)(2,1)} copy(bf16[2,64,1152]{2,1,0:T(8,128)(2,1)} %get-tuple-element.4) | data formatting | bytes 589824
  89.9 0.0 copy-done
  89.9 0.7 copy.11
Async XLA Ops:
  88.1 1.8 %copy-start = (bf16[2,64,1152]{2,1,0:T(8,128)(2,1)S(1)}, bf16[2,64,1152]{2,1,0:T(8,128)(2,1)}, u32[]{:S(2)}) copy-start(bf16[2,64,1152]{2,1,0:T(8,128)(2,1)} %get-tuple-element.5) | copy-start | bytes 884740

commit v3 on v2

--- a/solution.py
+++ b/solution.py
@@ -61,9 +61,9 @@
 
 
 def kernel(
-    q_hbm, k_hbm, v_hbm, stream_hbm, qt_hbm, kt_hbm, spatial_ref, temporal_ref,
-    staged, xt, rs, osend, orecv, qks, qkr, vs, vr, ts, tr, q_f, k_f, v_f, q_p, k_p, v_p, o_p,
-    send_x, recv_x, send_o, recv_o, send_qk, recv_qk, send_v, recv_v, send_t, recv_t, loads,
+    q_hbm, k_hbm, v_hbm, stream_hbm, qt_hbm, kt_hbm, spatial_hbm, temporal_hbm,
+    spatial_ref, temporal_ref, staged, xt, rs, osend, orecv, qks, qkr, vs, vr, ts, tr, q_f, k_f, v_f, q_p, k_p, v_p, o_p,
+    send_x, recv_x, send_o, recv_o, send_qk, recv_qk, send_v, recv_v, send_t, recv_t, loads, stores,
 ):
     s = lax.axis_index("space")
     t = lax.axis_index("tm")
@@ -282,6 +282,9 @@
         pack_v(j)
     start_far(vs, vr, send_v.at[1], recv_v.at[1], last_v)
     start_near(vs, vr, send_v.at[1], recv_v.at[1], last_v)
+
+    store_s = pltpu.make_async_copy(spatial_ref, spatial_hbm, stores.at[0])
+    store_s.start()
 
     to_position = one_hot(256, by_position)
     wait_tm(qkr, recv_qk)
@@ -346,9 +349,18 @@
     wait_tm(tr, recv_t.at[0], first_t)
     for j in range(2):
         unpack_t(j)
+    store_a = pltpu.make_async_copy(
+        temporal_ref.at[:, :, :512], temporal_hbm.at[:, :, :512], stores.at[1]
+    )
+    store_a.start()
     wait_tm(tr, recv_t.at[1], last_t)
     for j in range(2, 5):
         unpack_t(j)
+
+    store_b = pltpu.make_async_copy(
+        temporal_ref.at[:, :, 512:], temporal_hbm.at[:, :, 512:], stores.at[2]
+    )
+    store_b.start()
 
     def sent_o(i, c):
         p = lax.rem(s + i, NS)
@@ -361,6 +373,8 @@
         sent_tm(vs, send_v.at[n], part)
     for n, part in enumerate((first_t, last_t)):
         sent_tm(ts, send_t.at[n], part)
+    for copy in (store_s, store_a, store_b):
+        copy.wait()
 
 
 def per_device(*args):
@@ -371,8 +385,10 @@
         kernel,
         out_shape=(whole, whole),
         in_specs=[pl.BlockSpec(memory_space=pltpu.HBM)] * 6,
-        out_specs=(pl.BlockSpec(memory_space=vmem),) * 2,
+        out_specs=(pl.BlockSpec(memory_space=pltpu.HBM),) * 2,
         scratch_shapes=[
+            vmem((2, 64, D), BF),
+            vmem((2, 64, D), BF),
             vmem((6, 2, 64, D), BF),
             vmem((3, 144, 8, 128), BF),
             vmem((NS, 3, 9, 8, 128), BF),
@@ -395,6 +411,7 @@
             *[dma((NT,))] * 2,
             *[dma((2, NT))] * 4,
             dma((6,)),
+            dma((3,)),
         ],
         compiler_params=pltpu.CompilerParams(
             collective_id=0, has_side_effects=True, vmem_limit_bytes=60 * 2**20

time: 90.8 us -> 89.9 us (0.990)
  no operation moved by 1% of the time
where the time goes in v3:
time: 89.9 us; the launch traced here: 89.8 us
  Pallas kernels  86.7 us (96%)
  local copies, waits for them, and re-layouts  2.46 us (3%)
    pallas_call x1, Pallas kernels, per_device(): pl.pallas_call(kernel, out_shape=(whole, whole), in_specs=[pl.BlockSpec(m...  86.7 us
    unnamed x4, local copies, waits for them, and re-layouts  2.46 us

profile of v3, /device:TPU:1, one launch (start us, length us, event | category | flops | bytes accessed | tf_op | source)
XLA Modules:
  0.0 89.8 jit_solution(14131131468164306970)
XLA Ops:
  0.6 86.7 %attention.1 = (bf16[2,64,1152]{2,1,0:T(8,128)(2,1)}, bf16[2,64,1152]{2,1,0:T(8,128)(2,1)}) custom-call(bf16[2,64,1152]{2,1,0:T(8,128)(2,1)} %q_hbm.1, bf16[2,64,1152]{2,1,0:T(8,128)(2,1)} %k_hbm.1, bf16[2,64,1152]{2,1,0:T(8,128)(2,1)} %v_hbm.1, bf16[2,64,1152]{2,1,0:T(8,128)(2,1)} %stream_hbm.1, bf16[2,64,1152]{2,1,0:T(8,128)(2,1)} %qt_hbm.1, ...), custom_call_target="tpu_custom_call" | custom-call | flops 2000000000 | bytes 3000000 | tf_op jit(solution)/shard_map/attention/pallas_call | solution.py:384
  87.3 0.0 copy-start
  87.3 1.7 %copy.10 = bf16[2,64,1152]{2,1,0:T(8,128)(2,1)} copy(bf16[2,64,1152]{2,1,0:T(8,128)(2,1)} %get-tuple-element.4) | data formatting | bytes 589824
  89.0 0.0 copy-done
  89.1 0.7 copy.11
Async XLA Ops:
  87.3 1.8 %copy-start = (bf16[2,64,1152]{2,1,0:T(8,128)(2,1)S(1)}, bf16[2,64,1152]{2,1,0:T(8,128)(2,1)}, u32[]{:S(2)}) copy-start(bf16[2,64,1152]{2,1,0:T(8,128)(2,1)} %get-tuple-element.5) | copy-start | bytes 884740

commit v4 on v3

--- a/solution.py
+++ b/solution.py
@@ -144,6 +144,16 @@
             return c
 
         others(body)
+        pltpu.make_async_copy(src.at[t, part], dst.at[t, part], recv.at[t]).start()
+
+    def start_all(src, dst, send, recv, part):
+        def body(i, c):
+            tm_copy(src, dst, send, recv, far(i), t, part).start()
+            tm_copy(src, dst, send, recv, near(i), t, part).start()
+            return c
+
+        others(body)
+        tm_copy(src, dst, send, recv, far(14), t, part).start()
         pltpu.make_async_copy(src.at[t, part], dst.at[t, part], recv.at[t]).start()
 
     def wait_tm(dst, recv, part=slice(None)):
@@ -275,13 +285,11 @@
     start_far(qks, qkr, send_qk, recv_qk, low=8)
     for j in range(3):
         pack_v(j)
-    start_far(vs, vr, send_v.at[0], recv_v.at[0], first_v)
-    start_near(vs, vr, send_v.at[0], recv_v.at[0], first_v)
+    start_all(vs, vr, send_v.at[0], recv_v.at[0], first_v)
     lax.fori_loop(11, NS, wait_o, 0)
     for j in range(3, 5):
         pack_v(j)
-    start_far(vs, vr, send_v.at[1], recv_v.at[1], last_v)
-    start_near(vs, vr, send_v.at[1], recv_v.at[1], last_v)
+    start_all(vs, vr, send_v.at[1], recv_v.at[1], last_v)
 
     store_s = pltpu.make_async_copy(spatial_ref, spatial_hbm, stores.at[0])
     store_s.start()
@@ -323,8 +331,7 @@
         head(h)
     for j in range(2):
         pack_t(j)
-    start_far(ts, tr, send_t.at[0], recv_t.at[0], first_t)
-    start_near(ts, tr, send_t.at[0], recv_t.at[0], first_t)
+    start_all(ts, tr, send_t.at[0], recv_t.at[0], first_t)
     for h in range(8, 10):
         head(h)
     wait_tm(vr, recv_v.at[1], last_v)
@@ -334,8 +341,7 @@
         head(h)
     for j in range(2, 5):
         pack_t(j)
-    start_far(ts, tr, send_t.at[1], recv_t.at[1], last_t)
-    start_near(ts, tr, send_t.at[1], recv_t.at[1], last_t)
+    start_all(ts, tr, send_t.at[1], recv_t.at[1], last_t)
 
     from_peer = one_hot_t(256, by_peer)
 

time: 89.9 us -> 90.6 us (level)
  no operation moved by 1% of the time
where the time goes in v4:
time: 90.6 us; the launch traced here: 90.5 us
  Pallas kernels  87.4 us (96%)
  local copies, waits for them, and re-layouts  2.46 us (3%)
    pallas_call x1, Pallas kernels, per_device(): pl.pallas_call(kernel, out_shape=(whole, whole), in_specs=[pl.BlockSpec(m...  87.4 us
    unnamed x4, local copies, waits for them, and re-layouts  2.46 us

profile of v4, /device:TPU:1, one launch (start us, length us, event | category | flops | bytes accessed | tf_op | source)
XLA Modules:
  0.0 90.5 jit_solution(15205240630100880467)
XLA Ops:
  0.6 87.4 %attention.1 = (bf16[2,64,1152]{2,1,0:T(8,128)(2,1)}, bf16[2,64,1152]{2,1,0:T(8,128)(2,1)}) custom-call(bf16[2,64,1152]{2,1,0:T(8,128)(2,1)} %q_hbm.1, bf16[2,64,1152]{2,1,0:T(8,128)(2,1)} %k_hbm.1, bf16[2,64,1152]{2,1,0:T(8,128)(2,1)} %v_hbm.1, bf16[2,64,1152]{2,1,0:T(8,128)(2,1)} %stream_hbm.1, bf16[2,64,1152]{2,1,0:T(8,128)(2,1)} %qt_hbm.1, ...), custom_call_target="tpu_custom_call" | custom-call | flops 2000000000 | bytes 3000000 | tf_op jit(solution)/shard_map/attention/pallas_call | solution.py:390
  88.0 0.0 copy-start
  88.0 1.7 %copy.10 = bf16[2,64,1152]{2,1,0:T(8,128)(2,1)} copy(bf16[2,64,1152]{2,1,0:T(8,128)(2,1)} %get-tuple-element.4) | data formatting | bytes 589824
  89.8 0.0 copy-done
  89.8 0.7 copy.11
Async XLA Ops:
  88.0 1.8 %copy-start = (bf16[2,64,1152]{2,1,0:T(8,128)(2,1)S(1)}, bf16[2,64,1152]{2,1,0:T(8,128)(2,1)}, u32[]{:S(2)}) copy-start(bf16[2,64,1152]{2,1,0:T(8,128)(2,1)} %get-tuple-element.5) | copy-start | bytes 884740
